TPU v7x, 32 devices: a whole 2x2x4 slice. The times are simulated.
32 devices in a mesh: dist: 4 (over x, core), ctr: 8 (over z, y).
Axes of the slice: x: 2, y: 2, z: 4, core: 2. Of those that a mesh axis runs over, the one named last changes fastest.
Arguments:
- three_centre: bfloat16 [1024, 4, 4096], P(('dist', 'ctr')), may hold values from -0.359375 to 0.359375
- occupied_green: bfloat16 [128, 4096], P(('dist', 'ctr')), may hold values from -0.75 to 0.75
- virtual_green: bfloat16 [128, 4096], P(('dist', 'ctr')), may hold values from -0.75 to 0.75
- pair_index: int32 [16, 4], replicated, may hold values from 0 to 7, as said below
- source_slot: int32 [16, 4, 4], replicated, may hold values from -1 to 3, as said below
- occupied_index: int32 [16, 4, 4], replicated, may hold values from 0 to 127, as said below
- virtual_index: int32 [16, 4, 4], replicated, may hold values from 0 to 127, as said below
Outputs:
- density_response: float32 [1024, 256], P(('dist', 'ctr'))
Inputs may be any that keep to these rules, and one draw needn't show every extreme that they name: `pair_index`: the 4 entries of a row are distinct. `source_slot`: for each slot the listed slots are distinct and come first, followed by -1 entries; all slots of one auxiliary atom list the same number of slots, at least 1; in every draw some auxiliary atom lists 4. `occupied_index`: for auxiliary atom p with g = p // 4, every entry lies in g * 32 to g * 32 + 2 * 32 - 1, taken modulo 128. `virtual_index`: for auxiliary atom p with g = p // 4, every entry lies in g * 32 to g * 32 + 2 * 32 - 1, taken modulo 128.
All inputs are finite; a program needn't handle non-finite values.
Results may differ from a plain program's by a relative error of at most 0.004.
Values may be sent and summed in bfloat16 or wider, within the bound.
A program may use at most 64 MiB of HBM per device.

v0:
```python
import jax
import jax.numpy as jnp
from jax import lax
from jax.sharding import PartitionSpec as P

BLK = 64
AUXB = 64
NPR = 8


def shifted(block, axis, distance):
    devices = range(lax.axis_size(axis))
    route = [((i - distance) % len(devices), i) for i in devices]
    return lax.ppermute(block, axis, route)


def shards(
    three_centre,
    occupied_green,
    virtual_green,
    pair_index,
    source_slot,
    occupied_index,
    virtual_index,
):
    row_count = three_centre.shape[0]
    slot_count = three_centre.shape[1]
    ctr_size = lax.axis_size("ctr")
    dist_size = lax.axis_size("dist")
    dist_index = lax.axis_index("dist")
    ctr_index = lax.axis_index("ctr")
    flat_index = dist_index * ctr_size + ctr_index
    atom_index = flat_index * row_count // AUXB
    source_rows = lax.dynamic_index_in_dim(source_slot, atom_index, 0, keepdims=False)
    occ_ids = lax.dynamic_index_in_dim(occupied_index, atom_index, 0, keepdims=False)
    virt_ids = lax.dynamic_index_in_dim(virtual_index, atom_index, 0, keepdims=False)
    occ_own, virt_own = (
        lax.all_gather(occupied_green, "ctr", axis=0, tiled=True),
        lax.all_gather(virtual_green, "ctr", axis=0, tiled=True),
    )
    following = shifted(jnp.stack([occ_own, virt_own]), "dist", -1)
    occ_table = jnp.concatenate([occ_own, following[0]], axis=0)
    virt_table = jnp.concatenate([virt_own, following[1]], axis=0)
    region_base = dist_index * occ_own.shape[0]
    list_total = occ_own.shape[0] * dist_size
    occ_position = jnp.mod(occ_ids - region_base, list_total)
    virt_position = jnp.mod(virt_ids - region_base, list_total)
    tensor_rows = three_centre.reshape(row_count, slot_count, BLK, BLK)
    accumulated = jnp.zeros(tensor_rows.shape, jnp.float32)
    for step in range(source_rows.shape[1]):
        source_col = source_rows[:, step]
        live_mask = (source_col >= 0).astype(jnp.float32)
        picked = jnp.take(tensor_rows, jnp.maximum(source_col, 0), axis=1)
        virt_blocks = jnp.take(virt_table, virt_position[:, step], axis=0).reshape(
            slot_count, BLK, BLK
        )
        product = jnp.einsum(
            "aslv,svz->aslz", picked, virt_blocks, preferred_element_type=jnp.float32
        )
        product = (product * live_mask[None, :, None, None]).astype(jnp.bfloat16)
        occ_blocks = jnp.take(occ_table, occ_position[:, step], axis=0).reshape(
            slot_count, BLK, BLK
        )
        accumulated = accumulated + jnp.einsum(
            "slm,aslz->asmz", occ_blocks, product, preferred_element_type=jnp.float32
        )
    updated = accumulated.astype(jnp.bfloat16).reshape(row_count, slot_count, BLK * BLK)
    upd_region, ten_region = (
        lax.all_to_all(updated, "ctr", split_axis=2, concat_axis=0, tiled=True),
        lax.all_to_all(three_centre, "ctr", split_axis=2, concat_axis=0, tiled=True),
    )
    region_rows = upd_region.shape[0]
    col_count = upd_region.shape[2]
    region_atoms = region_rows // AUXB
    region_pairs = lax.dynamic_slice_in_dim(pair_index, dist_index * region_atoms, region_atoms, 0)
    one_hot = (region_pairs[:, :, None] == jnp.arange(NPR)[None, None, :]).astype(jnp.bfloat16)
    upd_blocks = upd_region.reshape(region_atoms, AUXB, slot_count, col_count)
    ten_blocks = ten_region.reshape(region_atoms, AUXB, slot_count, col_count)
    upd_space = (
        jnp.einsum("psk,pasc->kpac", one_hot, upd_blocks, preferred_element_type=jnp.float32)
        .astype(jnp.bfloat16)
        .reshape(NPR, region_rows, col_count)
    )
    ten_space = (
        jnp.einsum("psk,pasc->kpac", one_hot, ten_blocks, preferred_element_type=jnp.float32)
        .astype(jnp.bfloat16)
        .reshape(NPR, region_rows, col_count)
    )
    return lax.psum_scatter(
        jnp.einsum("kac,kbc->ab", upd_space, ten_space, preferred_element_type=jnp.float32),
        "ctr",
        scatter_dimension=0,
        tiled=True,
    )


def solution(mesh):
    return jax.shard_map(
        shards,
        mesh=mesh,
        in_specs=(
            P(("dist", "ctr"), None, None),
            P(("dist", "ctr"), None),
            P(("dist", "ctr"), None),
            P(),
            P(),
            P(),
            P(),
        ),
        out_specs=P(("dist", "ctr"), None),
        check_vma=False,
    )
```

profile of v0, /device:TPU:0, one launch (start us, length us, event | category | flops | bytes accessed | tf_op | source)
XLA Modules:
  0.0 265.6 jit_solution(9622120785204081876)
XLA Ops:
  6.5 32.9 %all-gather.1 = bf16[8,4,4096]{2,1,0:T(4,128)(2,1)S(1)} all-gather(bf16[1,4,4096]{2,1,0:T(4,128)(2,1)} %bitcast.126), channel_id=1, replica_groups=mesh['dist'=4,'ctr'=8] {'ctr'}, dimensions={0}, use_global_device_ids=true | all-gather | bytes 294912 | tf_op jit(solution)/shard_map/all_gather | solution.py:38
  39.4 30.9 %all-gather = bf16[8,4,4096]{2,1,0:T(4,128)(2,1)S(1)} all-gather(bf16[1,4,4096]{2,1,0:T(4,128)(2,1)} %bitcast.127), channel_id=1, replica_groups=mesh['dist'=4,'ctr'=8] {'ctr'}, dimensions={0}, use_global_device_ids=true | all-gather | bytes 294912 | tf_op jit(solution)/shard_map/all_gather | solution.py:39
  70.5 0.8 pad_maximum_fusion
  71.3 4.8 %copy.40 = bf16[32,4,4096]{0,1,2:T(4,128)(2,1)} copy(bf16[32,4,4096]{2,1,0:T(4,128)(2,1)S(1)} %copy-done.3) | data formatting | bytes 2097152 | tf_op args[0]
  76.2 7.8 %reshape.296 = bf16[8,2,32768]{2,1,0:T(2,128)(2,1)} reshape(bf16[4096,4,32]{2,1,0:T(4,128)(2,1)} %bitcast.120) | data formatting | bytes 2097152
  84.0 5.7 %all-to-all-start.1 = ((bf16[8,2,32768]{2,1,0:T(2,128)(2,1)}), bf16[8,2,32768]{2,1,0:T(2,128)(2,1)}, u32[]{:S(2)}, u32[]{:S(2)}) async-start(bf16[8,2,32768]{2,1,0:T(2,128)(2,1)} %reshape.296), calls=%async_computation.1 | async-start | bytes 2097152 | tf_op jit(solution)/shard_map/all_to_all | solution.py:70
  91.4 0.8 reshape.236
  92.2 1.8 reshape.108
  94.3 2.2 gather_fusion.10
  96.4 2.2 gather_fusion.7
  98.6 2.2 gather_fusion.4
  100.8 2.1 gather_fusion.1
  103.0 1.1 slice_bitcast_fusion
  104.0 1.0 pad_maximum_fusion.1
  105.1 0.6 gather_fusion.9
  111.5 4.7 %fusion.2 = f32[4,32,64,64]{3,2,1,0:T(8,128)} fusion(bf16[4,32,64,64]{3,2,1,0:T(8,128)(2,1)S(1)} %copy-done.2, f32[4]{0:T(128)S(1)} %get-tuple-element.18, pred[4]{0:T(512)(128)(4,1)S(1)} %get-tuple-element.41, bf16[4,64,64]{2,1,0:T(8,128)(2,1)S(1)} %reshape.112, bf16[4,64,64,1]{2,1,0,3:T(8,128)(2,1)S(1)} %reshape.268), kind=kOutput, calls=%fused_computation.19 | convolution fusion | flops 135790592 | bytes 3211284 | tf_op jit(solution)/shard_map/slm,aslz->asmz/dot_general | solution.py:64
  116.2 6.5 %fusion.8 = f32[4,32,64,64]{3,2,1,0:T(8,128)} fusion(bf16[4,32,64,64]{3,2,1,0:T(8,128)(2,1)} %gather_fusion.1, f32[4]{0:T(128)S(1)} %get-tuple-element.16, pred[4]{0:T(512)(128)(4,1)S(1)} %get-tuple-element.47, bf16[4,64,64]{2,1,0:T(8,128)(2,1)S(1)} %reshape.107, bf16[4,64,64,1]{2,1,0,3:T(8,128)(2,1)S(1)} %reshape.264), kind=kOutput, calls=%fused_computation.25 | convolution fusion | flops 135790592 | bytes 3211284 | tf_op jit(solution)/shard_map/slm,aslz->asmz/dot_general | solution.py:64
  122.6 4.7 %fusion.5 = f32[4,32,64,64]{3,2,1,0:T(8,128)} fusion(bf16[4,32,64,64]{3,2,1,0:T(8,128)(2,1)S(1)} %copy-done.1, f32[4]{0:T(128)S(1)} %get-tuple-element.17, pred[4]{0:T(512)(128)(4,1)S(1)} %get-tuple-element.44, bf16[4,64,64]{2,1,0:T(8,128)(2,1)S(1)} %reshape.110, bf16[4,64,64,1]{2,1,0,3:T(8,128)(2,1)S(1)} %reshape.266), kind=kOutput, calls=%fused_computation.22 | convolution fusion | flops 135790592 | bytes 3211284 | tf_op jit(solution)/shard_map/slm,aslz->asmz/dot_general | solution.py:64
  127.4 8.2 %fusion.22 = bf16[32,4,64,64]{2,3,0,1:T(8,128)(2,1)S(1)} fusion(f32[4,32,64,64]{3,2,1,0:T(8,128)} %fusion.2, f32[4,32,64,64]{3,2,1,0:T(8,128)} %fusion.8, f32[4,32,64,64]{3,2,1,0:T(8,128)} %fusion.5, bf16[4,32,64,64]{3,2,1,0:T(8,128)(2,1)} %gather_fusion.10, f32[4]{0:T(128)S(1)} %get-tuple-element.15, pred[4]{0:T(512)(128)(4,1)S(1)} %get-tuple-element.38, ...), kind=kOutput, calls=%fused_computation.41 | convolution fusion | flops 137887744 | bytes 8454164 | tf_op jit(solution)/shard_map/slm,aslz->asmz/dot_general | solution.py:64
  135.6 7.8 %copy.61 = bf16[32,4,64,64]{0,1,3,2:T(4,128)(2,1)} copy(bf16[32,4,64,64]{2,3,0,1:T(8,128)(2,1)S(1)} %fusion.22) | data formatting | bytes 2097152 | tf_op jit(solution)/shard_map/reshape | solution.py:67
  143.4 7.8 %reshape.298 = bf16[8,2,32768]{2,1,0:T(2,128)(2,1)} reshape(bf16[4096,4,32]{2,1,0:T(4,128)(2,1)} %bitcast.117) | data formatting | bytes 2097152
  151.2 6.1 %all-to-all-start = ((bf16[8,2,32768]{2,1,0:T(2,128)(2,1)}), bf16[8,2,32768]{2,1,0:T(2,128)(2,1)S(1)}, u32[]{:S(2)}, u32[]{:S(2)}) async-start(bf16[8,2,32768]{2,1,0:T(2,128)(2,1)} %reshape.298), calls=%async_computation | async-start | bytes 2097152 | tf_op jit(solution)/shard_map/all_to_all | solution.py:69
  157.6 7.0 %reshape.297 = bf16[4096,4,32]{2,1,0:T(4,128)(2,1)} reshape(bf16[8,2,32768]{2,1,0:T(2,128)(2,1)} %all-to-all-done.1) | data formatting | bytes 2097152
  164.6 6.1 %copy.41 = bf16[32,4,8,512]{3,1,0,2:T(4,128)(2,1)S(1)} copy(bf16[32,4,8,512]{0,1,3,2:T(4,128)(2,1)} %bitcast.118) | data formatting | bytes 2097152 | tf_op jit(solution)/shard_map/all_to_all | solution.py:70
  170.8 2.2 convolution_convert_fusion
  173.0 10.2 %all-to-all-done = bf16[8,2,32768]{2,1,0:T(2,128)(2,1)S(1)} async-done(((bf16[8,2,32768]{2,1,0:T(2,128)(2,1)}), bf16[8,2,32768]{2,1,0:T(2,128)(2,1)S(1)}, u32[]{:S(2)}, u32[]{:S(2)}) %all-to-all-start) | async-done | bytes 1048608 | tf_op jit(solution)/shard_map/all_to_all | solution.py:69
  183.2 4.5 %reshape.299 = bf16[4096,4,32]{2,1,0:T(4,128)(2,1)} reshape(bf16[8,2,32768]{2,1,0:T(2,128)(2,1)S(1)} %all-to-all-done) | data formatting | bytes 2097152
  187.8 4.7 %copy.62 = bf16[32,4,8,512]{3,2,0,1:T(8,128)(2,1)S(1)} copy(bf16[32,4,8,512]{0,1,3,2:T(4,128)(2,1)} %bitcast.119) | data formatting | bytes 2097152 | tf_op jit(solution)/shard_map/all_to_all | solution.py:69
  192.4 0.8 copy.38
  193.3 1.0 convolution_convert_fusion.1
  194.9 3.0 %fusion.41 = f32[256,256]{1,0:T(8,128)} fusion(bf16[8,256,512]{2,0,1:T(8,128)(2,1)S(1)} %bitcast.124, bf16[8,256,512]{2,0,1:T(8,128)(2,1)S(1)} %bitcast.125), kind=kOutput, calls=%fused_computation.42 | convolution fusion | flops 536870912 | bytes 4456448 | tf_op jit(solution)/shard_map/kac,kbc->ab/dot_general | solution.py:90
  197.9 60.9 %reduce-scatter.2.cloned.1.call-done = f32[32,256]{1,0:T(8,128)} async-done(((f32[256,256]{1,0:T(8,128)}), f32[32,256]{1,0:T(8,128)}) %reduce-scatter.2.cloned.1.call-update) | async-done | bytes 32784 | tf_op jit(solution)/shard_map/reduce_scatter | solution.py:89
  (82 shorter events, 8.4 us)
Async XLA Ops:
  6.5 83.2 %copy-start = (s32[16,4,4]{0,2,1:T(4,128)S(1)}, s32[16,4,4]{0,2,1:T(4,128)}, u32[]{:S(2)}) copy-start(s32[16,4,4]{0,2,1:T(4,128)} %param.15) | copy-start | bytes 3076
  6.5 64.8 %copy-start.3 = (bf16[32,4,4096]{2,1,0:T(4,128)(2,1)S(1)}, bf16[32,4,4096]{2,1,0:T(4,128)(2,1)}, u32[]{:S(2)}) copy-start(bf16[32,4,4096]{2,1,0:T(4,128)(2,1)} %param.11) | copy-start | bytes 3145732
  71.3 31.6 %collective-permute-start = (bf16[2,32,4096]{2,1,0:T(8,128)(2,1)}, bf16[2,32,4096]{2,1,0:T(8,128)(2,1)}, u32[]{:S(2)}, u32[]{:S(2)}) collective-permute-start(bf16[2,32,4096]{2,1,0:T(8,128)(2,1)} %pad_maximum_fusion), channel_id=1, source_target_pairs={{8,0},{16,8},{24,16},{0,24},{9,1},{17,9},{25,17},{1,25},{10,2},{18... | collective-permute-start | bytes 1572872 | tf_op jit(solution)/shard_map/ppermute | solution.py:14
  84.0 6.3 %copy-start.5 = (s32[16,4,4]{0,2,1:T(4,128)S(1)}, s32[16,4,4]{0,2,1:T(4,128)}, u32[]{:S(2)}) copy-start(s32[16,4,4]{0,2,1:T(4,128)} %param.16) | copy-start | bytes 3076
  84.0 6.8 %copy-start.6 = (s32[16,4,4]{0,2,1:T(4,128)S(1)}, s32[16,4,4]{0,2,1:T(4,128)}, u32[]{:S(2)}) copy-start(s32[16,4,4]{0,2,1:T(4,128)} %param.17) | copy-start | bytes 3076
  84.0 67.2 %all-to-all-start.1 = ((bf16[8,2,32768]{2,1,0:T(2,128)(2,1)}), bf16[8,2,32768]{2,1,0:T(2,128)(2,1)}, u32[]{:S(2)}, u32[]{:S(2)}) async-start(bf16[8,2,32768]{2,1,0:T(2,128)(2,1)} %reshape.296), calls=%async_computation.1 | async-start | bytes 2097152 | tf_op jit(solution)/shard_map/all_to_all | solution.py:70
  105.1 6.4 %copy-start.2 = (bf16[4,32,64,64]{3,2,1,0:T(8,128)(2,1)S(1)}, bf16[4,32,64,64]{3,2,1,0:T(8,128)(2,1)}, u32[]{:S(2)}) copy-start(bf16[4,32,64,64]{3,2,1,0:T(8,128)(2,1)} %gather_fusion.7) | copy-start | bytes 3145732
  116.2 6.5 %copy-start.1 = (bf16[4,32,64,64]{3,2,1,0:T(8,128)(2,1)S(1)}, bf16[4,32,64,64]{3,2,1,0:T(8,128)(2,1)}, u32[]{:S(2)}) copy-start(bf16[4,32,64,64]{3,2,1,0:T(8,128)(2,1)} %gather_fusion.4) | copy-start | bytes 3145732
  151.2 6.2 %copy-start.7 = (s32[16,4]{0,1:T(4,128)S(1)}, s32[16,4]{0,1:T(4,128)}, u32[]{:S(2)}) copy-start(s32[16,4]{0,1:T(4,128)} %param.14) | copy-start | bytes 772
  151.2 32.0 %all-to-all-start = ((bf16[8,2,32768]{2,1,0:T(2,128)(2,1)}), bf16[8,2,32768]{2,1,0:T(2,128)(2,1)S(1)}, u32[]{:S(2)}, u32[]{:S(2)}) async-start(bf16[8,2,32768]{2,1,0:T(2,128)(2,1)} %reshape.298), calls=%async_computation | async-start | bytes 2097152 | tf_op jit(solution)/shard_map/all_to_all | solution.py:69
  157.4 101.4 %reduce-scatter.2.cloned.1.call-start = ((), (), s32[]{:S(2)}) async-start(), calls=%async_computation.3 | async-start | bytes 294912 | tf_op jit(solution)/shard_map/reduce_scatter | solution.py:89
  193.3 1.6 copy-start.4
Sparse Core Ops, SparseCore 0:
  198.0 60.7 reduce-scatter.1
where the time goes:
time: 267 us; the launch traced here: 266 us
  waiting for transfers between devices  71.2 us (27%)
  local copies, waits for them, and re-layouts  71.1 us (27%)
  blocking collectives  63.8 us (24%)
  matrix products  30.3 us (11%)
  between operations  13.8 us (5%)
  starting transfers between devices  11.9 us (4%)
  other arithmetic  3.61 us (1%)
    reduce_scatter x1, waiting for transfers between devices, shards(): lax.psum_scatter(jnp.einsum('kac,kbc->ab', upd_space, ten_space, preferre...  60.9 us
    unnamed x23, local copies, waits for them, and re-layouts  33.5 us
    all_gather x1, blocking collectives, shards(): lax.all_gather(occupied_green, 'ctr', axis=0, tiled=True)  32.9 us
    all_gather x1, blocking collectives, shards(): lax.all_gather(virtual_green, 'ctr', axis=0, tiled=True)  30.9 us
    dot_general x4, matrix products, shards(): jnp.einsum('slm,aslz->asmz', occ_blocks, product, preferred_element_type=...  24.1 us
    all_to_all x1, waiting for transfers between devices, shards(): lax.all_to_all(updated, 'ctr', split_axis=2, concat_axis=0, tiled=True)  10.2 us
    gather x4, local copies, waits for them, and re-layouts, shards(): picked = jnp.take(tensor_rows, jnp.maximum(source_col, 0), axis=1)  8.66 us
    reshape x1, local copies, waits for them, and re-layouts, shards(): accumulated.astype(jnp.bfloat16).reshape(row_count, slot_count, BLK * BLK)  7.84 us
  transfers between devices with their start and end apart: 4, of which 2 were waited for; matrix products, arithmetic and copies ran while one was open for 34% of the time, Pallas kernels for 0%

commit v1 on v0

--- a/solution.py
+++ b/solution.py
@@ -66,7 +66,12 @@
         )
     updated = accumulated.astype(jnp.bfloat16).reshape(row_count, slot_count, BLK * BLK)
     upd_region, ten_region = (
-        lax.all_to_all(updated, "ctr", split_axis=2, concat_axis=0, tiled=True),
+        jnp.concatenate(
+            lax.all_to_all(
+                jnp.stack(jnp.split(updated, lax.axis_size("ctr"), axis=2)), "ctr", 0, 0
+            ),
+            axis=0,
+        ),
         lax.all_to_all(three_centre, "ctr", split_axis=2, concat_axis=0, tiled=True),
     )
     region_rows = upd_region.shape[0]

time: 267 us -> 251 us (0.940)
  local copies, waits for them, and re-layouts: 71.1 us -> 56.2 us
    unnamed x23 -> x30, local copies, waits for them, and re-layouts: 33.5 us -> 25.7 us
    reshape x1, local copies, waits for them, and re-layouts: 7.84 us -> 1.9 us  [shards(): accumulated.astype(jnp.bfloat16).reshape(row_count, slot_count, BLK * BLK)]
    all_to_all x2 -> x1, local copies, waits for them, and re-layouts: 5.47 us -> 0.82 us  [shards(): lax.all_to_all(jnp.stack(jnp.split(updated, lax.axis_size('ctr'), axis=2)...]
    convert_element_type x0 -> x1, local copies, waits for them, and re-layouts: none -> 3.07 us  [shards(): accumulated.astype(jnp.bfloat16).reshape(row_count, slot_count, BLK * BLK)]
  transfers between devices with their start and end apart: 4 -> 4, of which waited for: 2 -> 2; matrix products, arithmetic and copies ran while one was open for 34% -> 33% of each run, Pallas kernels for 0% -> 0%
where the time goes in v1:
time: 251 us; the launch traced here: 250 us
  waiting for transfers between devices  71.1 us (28%)
  blocking collectives  63.8 us (25%)
  local copies, waits for them, and re-layouts  56.2 us (22%)
  matrix products  31 us (12%)
  between operations  13.8 us (5%)
  starting transfers between devices  11.7 us (5%)
  other arithmetic  2.71 us (1%)
    reduce_scatter x1, waiting for transfers between devices, shards(): lax.psum_scatter(jnp.einsum('kac,kbc->ab', upd_space, ten_space, preferre...  60.9 us
    all_gather x1, blocking collectives, shards(): lax.all_gather(occupied_green, 'ctr', axis=0, tiled=True)  32.9 us
    all_gather x1, blocking collectives, shards(): lax.all_gather(virtual_green, 'ctr', axis=0, tiled=True)  30.9 us
    unnamed x30, local copies, waits for them, and re-layouts  25.7 us
    dot_general x4, matrix products, shards(): jnp.einsum('slm,aslz->asmz', occ_blocks, product, preferred_element_type=...  24.8 us
    all_to_all x1, waiting for transfers between devices, shards(): lax.all_to_all(jnp.stack(jnp.split(updated, lax.axis_size('ctr'), axis=2)...  10.2 us
    gather x4, local copies, waits for them, and re-layouts, shards(): picked = jnp.take(tensor_rows, jnp.maximum(source_col, 0), axis=1)  8.62 us
    all_to_all x1, local copies, waits for them, and re-layouts, shards(): lax.all_to_all(three_centre, 'ctr', split_axis=2, concat_axis=0, tiled=True)  6.13 us
  transfers between devices with their start and end apart: 4, of which 2 were waited for; matrix products, arithmetic and copies ran while one was open for 33% of the time, Pallas kernels for 0%

profile of v1, /device:TPU:0, one launch (start us, length us, event | category | flops | bytes accessed | tf_op | source)
XLA Modules:
  0.0 250.5 jit_solution(1862280302693868501)
XLA Ops:
  6.5 32.9 %all-gather.1 = bf16[8,4,4096]{2,1,0:T(4,128)(2,1)S(1)} all-gather(bf16[1,4,4096]{2,1,0:T(4,128)(2,1)} %bitcast.154), channel_id=1, replica_groups=mesh['dist'=4,'ctr'=8] {'ctr'}, dimensions={0}, use_global_device_ids=true | all-gather | bytes 294912 | tf_op jit(solution)/shard_map/all_gather | solution.py:38
  39.4 30.9 %all-gather = bf16[8,4,4096]{2,1,0:T(4,128)(2,1)S(1)} all-gather(bf16[1,4,4096]{2,1,0:T(4,128)(2,1)} %bitcast.155), channel_id=1, replica_groups=mesh['dist'=4,'ctr'=8] {'ctr'}, dimensions={0}, use_global_device_ids=true | all-gather | bytes 294912 | tf_op jit(solution)/shard_map/all_gather | solution.py:39
  70.5 0.9 pad_maximum_fusion
  71.4 4.8 %copy.36 = bf16[32,4,4096]{0,1,2:T(4,128)(2,1)} copy(bf16[32,4,4096]{2,1,0:T(4,128)(2,1)S(1)} %copy-done.3) | data formatting | bytes 2097152 | tf_op args[0]
  76.2 7.8 %reshape.291 = bf16[8,2,32768]{2,1,0:T(2,128)(2,1)} reshape(bf16[4096,4,32]{2,1,0:T(4,128)(2,1)} %bitcast.149) | data formatting | bytes 2097152
  84.1 5.7 %all-to-all-start.1 = ((bf16[8,2,32768]{2,1,0:T(2,128)(2,1)}), bf16[8,2,32768]{2,1,0:T(2,128)(2,1)}, u32[]{:S(2)}, u32[]{:S(2)}) async-start(bf16[8,2,32768]{2,1,0:T(2,128)(2,1)} %reshape.291), calls=%async_computation.1 | async-start | bytes 2097152 | tf_op jit(solution)/shard_map/all_to_all | solution.py:75
  91.5 0.8 reshape.231
  92.3 1.6 reshape.104
  94.1 2.2 gather_fusion.10
  96.3 2.1 gather_fusion.7
  98.4 2.1 gather_fusion.4
  100.6 2.2 gather_fusion.1
  102.8 1.1 slice_bitcast_fusion
  110.4 6.4 %fusion.2 = f32[4,32,64,64]{3,2,1,0:T(8,128)} fusion(bf16[4,32,64,64]{3,2,1,0:T(8,128)(2,1)} %gather_fusion.7, f32[4]{0:T(128)S(1)} %get-tuple-element.18, pred[4]{0:T(512)(128)(4,1)S(1)} %get-tuple-element.41, bf16[4,64,64]{2,1,0:T(8,128)(2,1)S(1)} %reshape.108, bf16[4,64,64,1]{2,1,0,3:T(8,128)(2,1)S(1)} %reshape.263), kind=kOutput, calls=%fused_computation.19 | convolution fusion | flops 135790592 | bytes 3211284 | tf_op jit(solution)/shard_map/slm,aslz->asmz/dot_general | solution.py:64
  116.8 4.7 %fusion.8 = f32[4,32,64,64]{3,2,1,0:T(8,128)} fusion(bf16[4,32,64,64]{3,2,1,0:T(8,128)(2,1)S(1)} %copy-done.2, f32[4]{0:T(128)S(1)} %get-tuple-element.16, pred[4]{0:T(512)(128)(4,1)S(1)} %get-tuple-element.47, bf16[4,64,64]{2,1,0:T(8,128)(2,1)S(1)} %reshape.103, bf16[4,64,64,1]{2,1,0,3:T(8,128)(2,1)S(1)} %reshape.259), kind=kOutput, calls=%fused_computation.25 | convolution fusion | flops 135790592 | bytes 3211284 | tf_op jit(solution)/shard_map/slm,aslz->asmz/dot_general | solution.py:64
  121.5 6.5 %fusion.5 = f32[4,32,64,64]{3,2,1,0:T(8,128)} fusion(bf16[4,32,64,64]{3,2,1,0:T(8,128)(2,1)} %gather_fusion.4, f32[4]{0:T(128)S(1)} %get-tuple-element.17, pred[4]{0:T(512)(128)(4,1)S(1)} %get-tuple-element.44, bf16[4,64,64]{2,1,0:T(8,128)(2,1)S(1)} %reshape.106, bf16[4,64,64,1]{2,1,0,3:T(8,128)(2,1)S(1)} %reshape.261), kind=kOutput, calls=%fused_computation.22 | convolution fusion | flops 135790592 | bytes 3211284 | tf_op jit(solution)/shard_map/slm,aslz->asmz/dot_general | solution.py:64
  128.0 7.2 %fusion.22 = bf16[32,4,64,64]{2,3,0,1:T(8,128)(2,1)} fusion(f32[4,32,64,64]{3,2,1,0:T(8,128)} %fusion.2, f32[4,32,64,64]{3,2,1,0:T(8,128)} %fusion.8, f32[4,32,64,64]{3,2,1,0:T(8,128)} %fusion.5, bf16[4,32,64,64]{3,2,1,0:T(8,128)(2,1)S(1)} %copy-done.1, f32[4]{0:T(128)S(1)} %get-tuple-element.15, pred[4]{0:T(512)(128)(4,1)S(1)} %get-tuple-element.38, ...), kind=kOutput, calls=%fused_computation.41 | convolution fusion | flops 137887744 | bytes 8454164 | tf_op jit(solution)/shard_map/slm,aslz->asmz/dot_general | solution.py:64
  135.1 3.1 %copy.33 = bf16[32,4,64,64]{3,2,0,1:T(8,128)(2,1)S(1)} copy(bf16[32,4,64,64]{2,3,0,1:T(8,128)(2,1)} %fusion.22) | data formatting | bytes 2097152 | tf_op jit(solution)/shard_map/convert_element_type | solution.py:67
  138.2 1.9 reshape.112
  142.1 0.7 fusion.59
  142.8 0.7 fusion.58
  143.4 0.7 fusion.57
  144.7 0.7 fusion.55
  145.4 6.0 %all-to-all-start = ((bf16[8,32,4,512]{3,1,2,0:T(8,128)(2,1)}), bf16[8,32,4,512]{3,1,2,0:T(8,128)(2,1)S(1)}, u32[]{:S(2)}, u32[]{:S(2)}) async-start(bf16[8,32,4,512]{3,1,2,0:T(8,128)(2,1)} %fusion.55), calls=%async_computation | async-start | bytes 2097152 | tf_op jit(solution)/shard_map/all_to_all | solution.py:70
  151.6 7.0 %reshape.292 = bf16[4096,4,32]{2,1,0:T(4,128)(2,1)} reshape(bf16[8,2,32768]{2,1,0:T(2,128)(2,1)} %all-to-all-done.1) | data formatting | bytes 2097152
  158.7 6.1 %copy.37 = bf16[32,4,8,512]{3,1,0,2:T(4,128)(2,1)S(1)} copy(bf16[32,4,8,512]{0,1,3,2:T(4,128)(2,1)} %bitcast.148) | data formatting | bytes 2097152 | tf_op jit(solution)/shard_map/all_to_all | solution.py:75
  164.8 2.3 convolution_convert_fusion
  167.1 10.2 %all-to-all-done = bf16[8,32,4,512]{3,1,2,0:T(8,128)(2,1)S(1)} async-done(((bf16[8,32,4,512]{3,1,2,0:T(8,128)(2,1)}), bf16[8,32,4,512]{3,1,2,0:T(8,128)(2,1)S(1)}, u32[]{:S(2)}, u32[]{:S(2)}) %all-to-all-start) | async-done | bytes 1048608 | tf_op jit(solution)/shard_map/all_to_all | solution.py:70
  177.3 0.8 copy.34
  178.1 1.0 convolution_convert_fusion.1
  179.7 3.0 %fusion.41 = f32[256,256]{1,0:T(8,128)} fusion(bf16[8,256,512]{2,0,1:T(8,128)(2,1)S(1)} %bitcast.152, bf16[8,256,512]{2,0,1:T(8,128)(2,1)S(1)} %bitcast.153), kind=kOutput, calls=%fused_computation.42 | convolution fusion | flops 536870912 | bytes 4456448 | tf_op jit(solution)/shard_map/kac,kbc->ab/dot_general | solution.py:95
  182.7 60.9 %reduce-scatter.2.cloned.1.call-done = f32[32,256]{1,0:T(8,128)} async-done(((f32[256,256]{1,0:T(8,128)}), f32[32,256]{1,0:T(8,128)}) %reduce-scatter.2.cloned.1.call-update) | async-done | bytes 32784 | tf_op jit(solution)/shard_map/reduce_scatter | solution.py:94
  (90 shorter events, 11.7 us)
Async XLA Ops:
  6.5 83.2 %copy-start = (s32[16,4,4]{0,2,1:T(4,128)S(1)}, s32[16,4,4]{0,2,1:T(4,128)}, u32[]{:S(2)}) copy-start(s32[16,4,4]{0,2,1:T(4,128)} %param.15) | copy-start | bytes 3076
  6.5 64.9 %copy-start.3 = (bf16[32,4,4096]{2,1,0:T(4,128)(2,1)S(1)}, bf16[32,4,4096]{2,1,0:T(4,128)(2,1)}, u32[]{:S(2)}) copy-start(bf16[32,4,4096]{2,1,0:T(4,128)(2,1)} %param.11) | copy-start | bytes 3145732
  71.4 31.4 %collective-permute-start = (bf16[2,32,4096]{2,1,0:T(8,128)(2,1)}, bf16[2,32,4096]{2,1,0:T(8,128)(2,1)}, u32[]{:S(2)}, u32[]{:S(2)}) collective-permute-start(bf16[2,32,4096]{2,1,0:T(8,128)(2,1)} %pad_maximum_fusion), channel_id=1, source_target_pairs={{8,0},{16,8},{24,16},{0,24},{9,1},{17,9},{25,17},{1,25},{10,2},{18... | collective-permute-start | bytes 1572872 | tf_op jit(solution)/shard_map/ppermute | solution.py:14
  84.0 6.3 %copy-start.6 = (s32[16,4,4]{0,2,1:T(4,128)S(1)}, s32[16,4,4]{0,2,1:T(4,128)}, u32[]{:S(2)}) copy-start(s32[16,4,4]{0,2,1:T(4,128)} %param.16) | copy-start | bytes 3076
  84.1 6.8 %copy-start.7 = (s32[16,4,4]{0,2,1:T(4,128)S(1)}, s32[16,4,4]{0,2,1:T(4,128)}, u32[]{:S(2)}) copy-start(s32[16,4,4]{0,2,1:T(4,128)} %param.17) | copy-start | bytes 3076
  84.1 61.4 %all-to-all-start.1 = ((bf16[8,2,32768]{2,1,0:T(2,128)(2,1)}), bf16[8,2,32768]{2,1,0:T(2,128)(2,1)}, u32[]{:S(2)}, u32[]{:S(2)}) async-start(bf16[8,2,32768]{2,1,0:T(2,128)(2,1)} %reshape.291), calls=%async_computation.1 | async-start | bytes 2097152 | tf_op jit(solution)/shard_map/all_to_all | solution.py:75
  100.6 3.3 %copy-start.5 = (bf16[32,4096]{1,0:T(8,128)(2,1)S(1)}, bf16[32,4096]{1,0:T(8,128)(2,1)}, u32[]{:S(2)}) copy-start(bf16[32,4096]{1,0:T(8,128)(2,1)} %reshape.231) | copy-start | bytes 786436
  110.3 6.4 %copy-start.2 = (bf16[4,32,64,64]{3,2,1,0:T(8,128)(2,1)S(1)}, bf16[4,32,64,64]{3,2,1,0:T(8,128)(2,1)}, u32[]{:S(2)}) copy-start(bf16[4,32,64,64]{3,2,1,0:T(8,128)(2,1)} %gather_fusion.1) | copy-start | bytes 3145732
  121.5 6.5 %copy-start.1 = (bf16[4,32,64,64]{3,2,1,0:T(8,128)(2,1)S(1)}, bf16[4,32,64,64]{3,2,1,0:T(8,128)(2,1)}, u32[]{:S(2)}) copy-start(bf16[4,32,64,64]{3,2,1,0:T(8,128)(2,1)} %gather_fusion.10) | copy-start | bytes 3145732
  140.1 11.3 %copy-start.8 = (s32[16,4]{0,1:T(4,128)S(1)}, s32[16,4]{0,1:T(4,128)}, u32[]{:S(2)}) copy-start(s32[16,4]{0,1:T(4,128)} %param.14) | copy-start | bytes 772
  145.4 31.9 %all-to-all-start = ((bf16[8,32,4,512]{3,1,2,0:T(8,128)(2,1)}), bf16[8,32,4,512]{3,1,2,0:T(8,128)(2,1)S(1)}, u32[]{:S(2)}, u32[]{:S(2)}) async-start(bf16[8,32,4,512]{3,1,2,0:T(8,128)(2,1)} %fusion.55), calls=%async_computation | async-start | bytes 2097152 | tf_op jit(solution)/shard_map/all_to_all | solution.py:70
  151.4 92.2 %reduce-scatter.2.cloned.1.call-start = ((), (), s32[]{:S(2)}) async-start(), calls=%async_computation.3 | async-start | bytes 294912 | tf_op jit(solution)/shard_map/reduce_scatter | solution.py:94
  178.1 1.6 copy-start.4
Sparse Core Ops, SparseCore 0:
  182.8 60.7 reduce-scatter.1
